TPU v7x, 256 devices: a whole 4x4x8 slice. The times are simulated.
256 devices in a mesh: tup: 32 (over z, y), lang: 8 (over x, core).
Axes of the slice: x: 4, y: 4, z: 8, core: 2. Of those that a mesh axis runs over, the one named last changes fastest.
Arguments:
- counts: bfloat16 [8, 4096, 16384], P('lang', 'tup'), may hold values from 0 to 80
- lengths: int32 [8, 4096], P('lang', 'tup'), may hold values from 96 to 128, as said below
- tuple_map: int32 [8, 4096], P('lang', 'tup'), may hold values from 0 to 4095, as said below
- topic_mix: bfloat16 [4096, 256], P('tup'), may hold values from 0.049804688 to 5
- word_probs: bfloat16 [8, 16384, 256], P('lang', 'tup'), may hold values from 0.099609375 to 10
Outputs:
- mix_update: float32 [4096, 256], P('tup')
- word_update: float32 [8, 16384, 256], P('lang', 'tup')
Inputs may be any that keep to these rules, and one draw needn't show every extreme that they name: `lengths`: the first row of every language spans all 128 tiles. `tuple_map`: each language names every tuple once; the 128 rows of one index of tup hold exactly 4 tuples t of each value of t // 128.
All inputs are finite; a program needn't handle non-finite values.
Results may differ from a plain program's by a relative error of at most 0.0003.
Values may be sent and summed in bfloat16 or wider, within the bound.
No kernel may reach another device: no remote copies, remote signals or barrier semaphores. Data moves between devices by JAX's collectives and lax.ppermute only.
A program may use at most 128 MiB of HBM per device.

v0:
```python
import math
import jax
import jax.numpy as jnp
from jax import lax
from jax.sharding import PartitionSpec as P


def ratio_block(count_block, mix_block, word_block):
    expected = lax.dot_general(
        mix_block, word_block, (((1,), (1,)), ((), ())), preferred_element_type=jnp.float32
    )
    return count_block.astype(jnp.float32) / expected


def topic_term(ratios, word_block):
    return jnp.dot(ratios, word_block.astype(jnp.float32), precision=lax.Precision.HIGHEST)


def word_term(ratios, mix_rows):
    return lax.dot_general(
        ratios,
        mix_rows.astype(jnp.float32),
        (((0,), (0,)), ((), ())),
        precision=lax.Precision.HIGHEST,
    )


def ratio_pass(row_counts, mix_rows, word_local):
    shard_len = word_local.shape[0]
    topics = word_local.shape[1]
    vocab_size = shard_len * lax.axis_size("tup")
    topic_zero = jnp.zeros((row_counts.shape[0], topics), jnp.float32)
    shard_rows = lax.all_gather(word_local, "tup", axis=0, tiled=True)
    row_span = shard_rows.shape[0]
    block_len = math.gcd(row_span, 2048)

    def block_step(block_index, inner_pair):
        topic_sum, word_sum = inner_pair
        begin_row = block_index * block_len
        word_block = lax.dynamic_slice_in_dim(shard_rows, begin_row, block_len, 0)
        count_block = lax.dynamic_slice_in_dim(row_counts, begin_row, block_len, 1)
        ratios = ratio_block(count_block, mix_rows, word_block)
        topic_sum = topic_sum + topic_term(ratios, word_block)
        word_sum = lax.dynamic_update_slice_in_dim(
            word_sum, word_term(ratios, mix_rows), begin_row, 0
        )
        return (topic_sum, word_sum)

    topic_sum, word_sum = lax.fori_loop(
        0,
        row_span // block_len,
        block_step,
        (topic_zero, jnp.zeros((vocab_size, topics), jnp.float32)),
    )
    return (topic_sum, lax.psum_scatter(word_sum, "tup", scatter_dimension=0, tiled=True))


def on_device(counts, lengths, tuple_map, topic_mix, word_probs):
    count_rows = counts[0]
    tup_rows, vocab_size = count_rows.shape
    topics = topic_mix.shape[1]
    groups = lax.axis_size("tup")
    per_owner = tup_rows // groups
    tile_of = jnp.arange(vocab_size, dtype=jnp.int32) // 128
    live_counts = count_rows * (tile_of[None, :] < lengths[0][:, None]).astype(jnp.bfloat16)
    tuple_ids = tuple_map[0]
    word_local = word_probs[0]
    bucket_order = jnp.argsort(tuple_ids // tup_rows, stable=True)
    bucket_ids = tuple_ids[bucket_order].reshape(groups, per_owner)
    arrived = lax.all_to_all(
        live_counts[bucket_order].reshape(groups, per_owner, vocab_size),
        "tup",
        split_axis=0,
        concat_axis=0,
        tiled=True,
    ).reshape(tup_rows, vocab_size)
    arrived_ids = lax.all_to_all(
        bucket_ids, "tup", split_axis=0, concat_axis=0, tiled=True
    ).reshape(tup_rows)
    local_ids = arrived_ids % tup_rows
    mix_rows = topic_mix[local_ids]
    topic_sum, word_sum = ratio_pass(arrived, mix_rows, word_local)
    placed = jnp.zeros_like(topic_sum).at[local_ids].set(topic_sum)
    totals = lax.psum(placed, "lang")
    mixed = topic_mix.astype(jnp.float32) * totals
    mix_update = topics * mixed / jnp.sum(mixed, 1, keepdims=True)
    scaled = word_local.astype(jnp.float32) * word_sum
    column = lax.psum(jnp.sum(scaled, 0), "tup")
    word_update = (vocab_size * scaled / column[None, :])[None]
    return (mix_update, word_update)


def solution(mesh):
    return jax.shard_map(
        on_device,
        mesh=mesh,
        in_specs=(
            P("lang", "tup", None),
            P("lang", "tup"),
            P("lang", "tup"),
            P("tup", None),
            P("lang", "tup", None),
        ),
        out_specs=(P("tup", None), P("lang", "tup", None)),
        check_vma=False,
    )
```

profile of v0, /device:TPU:4, one launch (start us, length us, event | category | flops | bytes accessed | tf_op | source)
XLA Modules:
  0.0 659.9 jit_solution(987465419086488916)
XLA Ops:
  7.2 0.7 all-gather.3.cloned.1.call-update
  7.9 0.7 and_select_fusion.1
  8.6 2.5 sort.17
  11.1 1.6 gather_fusion
  12.7 0.7 all_to_all.9
  13.4 11.5 %all-to-all-start = ((s32[32,1,4]{2,1,0:T(1,128)}), s32[32,1,4]{2,1,0:T(1,128)S(1)}, u32[]{:S(2)}, u32[]{:S(2)}) async-start(s32[32,1,4]{2,1,0:T(1,128)} %bitcast.1), calls=%async_computation | async-start | bytes 32768 | tf_op jit(solution)/shard_map/all_to_all | solution.py:77
  24.9 5.4 compare_select_fusion
  30.3 11.5 %gather_fusion.1 = bf16[128,16384]{1,0:T(8,128)(2,1)} fusion(bf16[128,16384]{1,0:T(8,128)(2,1)} %compare_select_fusion, s32[1024]{0:T(1024)S(1)} %pad_clamp_fusion.1), kind=kCustom, calls=%fused_computation.1 | custom fusion | bytes 8389120 | tf_op jit(solution)/shard_map/gather | solution.py:71
  41.8 7.2 %reshape.96 = bf16[32,4,16384]{2,1,0:T(4,128)(2,1)} reshape(bf16[128,16384]{1,0:T(8,128)(2,1)} %gather_fusion.1) | data formatting | bytes 8388608 | tf_op jit(solution)/shard_map/reshape | solution.py:71
  49.1 10.0 %all-to-all-start.1 = ((bf16[32,4,16384]{2,1,0:T(4,128)(2,1)}), bf16[32,4,16384]{2,1,0:T(4,128)(2,1)}, u32[]{:S(2)}, u32[]{:S(2)}) async-start(bf16[32,4,16384]{2,1,0:T(4,128)(2,1)} %reshape.96), calls=%async_computation.1 | async-start | bytes 8388608 | tf_op jit(solution)/shard_map/all_to_all | solution.py:70
  59.4 0.5 broadcast.129
  59.9 0.7 reduce.3
  60.7 0.8 gather_fusion.2
  61.6 130.7 %all-to-all-done.1 = bf16[32,4,16384]{2,1,0:T(4,128)(2,1)} async-done(((bf16[32,4,16384]{2,1,0:T(4,128)(2,1)}), bf16[32,4,16384]{2,1,0:T(4,128)(2,1)}, u32[]{:S(2)}, u32[]{:S(2)}) %all-to-all-start.1) | async-done | bytes 4194336 | tf_op jit(solution)/shard_map/all_to_all | solution.py:70
  192.2 6.9 %reshape.97 = bf16[128,16384]{1,0:T(8,128)(2,1)} reshape(bf16[32,4,16384]{2,1,0:T(4,128)(2,1)} %all-to-all-done.1) | data formatting | bytes 8388608 | tf_op jit(solution)/shard_map/reshape | solution.py:76
  199.2 6.0 broadcast_in_dim.7
  205.2 60.9 %while.16 = (s32[]{:T(128)}, f32[128,256]{1,0:T(8,128)S(1)}, f32[16384,256]{1,0:T(8,128)}, bf16[128,16384]{1,0:T(8,128)(2,1)}, bf16[16384,256]{1,0:T(8,128)(2,1)...) while((s32[]{:T(128)}, f32[128,256]{1,0:T(8,128)S(1)}, ...), condition=%wide.region_2.3_spmd.clone, body=%wide.region_1.2_spmd.clone.sunk | while | flops 1745420288 | bytes 10354869 | solution.py:49
  205.2 1.1 constant_dynamic-slice_fusion.2
  206.2 0.3 copy.13
  206.5 1.7 fusion.31
  208.2 2.3 convolution_add_fusion.2
  210.4 2.3 convolution_dynamic-update-slice_fusion.2
  212.8 1.1 constant_dynamic-slice_fusion.2
  213.9 0.3 copy.13
  214.1 1.7 fusion.31
  215.8 2.3 convolution_add_fusion.2
  218.1 2.3 convolution_dynamic-update-slice_fusion.2
  220.3 1.1 constant_dynamic-slice_fusion.2
  221.4 0.3 copy.13
  221.7 1.7 fusion.31
  223.4 2.3 convolution_add_fusion.2
  225.6 2.3 convolution_dynamic-update-slice_fusion.2
  227.9 1.1 constant_dynamic-slice_fusion.2
  229.0 0.3 copy.13
  229.3 1.7 fusion.31
  231.0 2.3 convolution_add_fusion.2
  233.2 2.3 convolution_dynamic-update-slice_fusion.2
  235.6 1.1 constant_dynamic-slice_fusion.2
  236.6 0.3 copy.13
  236.9 1.7 fusion.31
  238.6 2.3 convolution_add_fusion.2
  240.9 2.4 convolution_dynamic-update-slice_fusion.2
  243.2 1.1 constant_dynamic-slice_fusion.2
  244.3 0.3 copy.13
  244.6 1.7 fusion.31
  246.3 2.3 convolution_add_fusion.2
  248.5 2.3 convolution_dynamic-update-slice_fusion.2
  250.8 1.1 constant_dynamic-slice_fusion.2
  252.2 1.7 fusion.31
  253.8 2.3 convolution_add_fusion.2
  256.1 2.3 convolution_dynamic-update-slice_fusion.2
  258.4 1.1 constant_dynamic-slice_fusion.2
  259.8 1.7 fusion.31
  261.5 2.3 convolution_add_fusion.2
  263.7 2.3 convolution_dynamic-update-slice_fusion.2
  266.0 1.6 scatter_custom_fusion
  267.7 0.7 reduce-scatter.2.cloned.1.call-update
  268.4 57.4 %all-reduce.2.cloned.1.call-done = f32[128,256]{1,0:T(8,128)} async-done(((f32[128,256]{1,0:T(8,128)}), f32[128,256]{1,0:T(8,128)}) %all-reduce.2.cloned.1.call-update) | async-done | bytes 131088 | tf_op jit(solution)/shard_map/psum | solution.py:84
  325.8 1.0 fusion.6
  326.8 1.7 multiply_divide_fusion
  328.5 249.4 %reduce-scatter.2.cloned.1.call-done = f32[512,256]{1,0:T(8,128)} async-done(((f32[16384,256]{1,0:T(8,128)}), f32[512,256]{1,0:T(8,128)}) %reduce-scatter.2.cloned.1.call-update) | async-done | bytes 524304 | tf_op jit(solution)/shard_map/reduce_scatter | solution.py:55
  577.9 1.1 fusion.5
  579.1 72.4 %psum.15 = f32[256]{0:T(256)S(1)} all-reduce(f32[256]{0:T(256)S(1)} %fusion.5), channel_id=1, replica_groups=mesh['tup'=32,'lang'=8] {'tup'}, use_global_device_ids=true, to_apply=%region_8.9 | all-reduce | flops 256 | bytes 2048 | tf_op jit(solution)/shard_map/psum | solution.py:88
  651.5 1.9 divide_bitcast_fusion
  (20 shorter events, 1.0 us)
Async XLA Ops:
  7.2 192.0 %all-gather.3.cloned.1.call-start = ((), (), s32[]{:S(2)}) async-start(), calls=%async_computation.5 | async-start | bytes 8650752 | tf_op jit(solution)/shard_map/all_gather | solution.py:33
  13.4 35.6 %all-to-all-start = ((s32[32,1,4]{2,1,0:T(1,128)}), s32[32,1,4]{2,1,0:T(1,128)S(1)}, u32[]{:S(2)}, u32[]{:S(2)}) async-start(s32[32,1,4]{2,1,0:T(1,128)} %bitcast.1), calls=%async_computation | async-start | bytes 32768 | tf_op jit(solution)/shard_map/all_to_all | solution.py:77
  49.1 11.6 %copy-start = (bf16[128,256]{1,0:T(8,128)(2,1)S(1)}, bf16[128,256]{1,0:T(8,128)(2,1)}, u32[]{:S(2)}) copy-start(bf16[128,256]{1,0:T(8,128)(2,1)} %param.10) | copy-start | bytes 196612
  49.1 143.2 %all-to-all-start.1 = ((bf16[32,4,16384]{2,1,0:T(4,128)(2,1)}), bf16[32,4,16384]{2,1,0:T(4,128)(2,1)}, u32[]{:S(2)}, u32[]{:S(2)}) async-start(bf16[32,4,16384]{2,1,0:T(4,128)(2,1)} %reshape.96), calls=%async_computation.1 | async-start | bytes 8388608 | tf_op jit(solution)/shard_map/all_to_all | solution.py:70
  59.1 266.7 %all-reduce.2.cloned.1.call-start = ((), (), s32[]{:S(2)}) async-start(), calls=%async_computation.3 | async-start | bytes 262144 | tf_op jit(solution)/shard_map/psum | solution.py:84
  267.7 310.2 %reduce-scatter.2.cloned.1.call-start = ((), (), s32[]{:S(2)}) async-start(), calls=%async_computation.4 | async-start | bytes 17301504 | tf_op jit(solution)/shard_map/reduce_scatter | solution.py:55
  267.7 310.2 %copy-start.1 = (bf16[1,512,256]{2,1,0:T(8,128)(2,1)S(1)}, bf16[1,512,256]{2,1,0:T(8,128)(2,1)}, u32[]{:S(2)}) copy-start(bf16[1,512,256]{2,1,0:T(8,128)(2,1)} %param.11) | copy-start | bytes 786436
Sparse Core Ops, SparseCore 0:
  10.6 176.9 all-gather.2
  267.8 57.9 all-reduce.1
  330.5 247.3 reduce-scatter.1
where the time goes:
time: 662 us; the launch traced here: 660 us
  waiting for transfers between devices  439 us (66%)
  blocking collectives  72.4 us (11%)
  matrix products  49.9 us (8%)
  local copies, waits for them, and re-layouts  47.8 us (7%)
  starting transfers between devices  21.8 us (3%)
  other arithmetic  15.1 us (2%)
  between operations  13.8 us (2%)
    reduce_scatter x1, waiting for transfers between devices, ratio_pass(): lax.psum_scatter(word_sum, 'tup', scatter_dimension=0, tiled=True)  249 us
    all_to_all x1, waiting for transfers between devices, on_device(): lax.all_to_all(live_counts[bucket_order].reshape(groups, per_owner, vocab...  131 us
    psum x1, blocking collectives, on_device(): column = lax.psum(jnp.sum(scaled, 0), 'tup')  72.4 us
    psum x1, waiting for transfers between devices, on_device(): totals = lax.psum(placed, 'lang')  57.4 us
    dot_general x8, matrix products, word_term(): lax.dot_general(ratios, mix_rows.astype(jnp.float32), (((0,), (0,)), ((),...  18.6 us
    dot_general x8, matrix products, topic_term(): jnp.dot(ratios, word_block.astype(jnp.float32), precision=lax.Precision.H...  18 us
    dot_general x8, matrix products, ratio_block(): lax.dot_general(mix_block, word_block, (((1,), (1,)), ((), ())), preferre...  13.3 us
  transfers between devices with their start and end apart: 5, of which 3 were waited for; matrix products, arithmetic and copies ran while one was open for 6% of the time, Pallas kernels for 0%

commit v1 on v0

--- a/solution.py
+++ b/solution.py
@@ -85,7 +85,9 @@
     mixed = topic_mix.astype(jnp.float32) * totals
     mix_update = topics * mixed / jnp.sum(mixed, 1, keepdims=True)
     scaled = word_local.astype(jnp.float32) * word_sum
-    column = lax.psum(jnp.sum(scaled, 0), "tup")
+    own = jnp.sum(scaled, 0)
+    parts = lax.all_gather(own, "tup")
+    column = jnp.sum(parts, axis=0)
     word_update = (vocab_size * scaled / column[None, :])[None]
     return (mix_update, word_update)
 

time: 662 us -> 631 us (0.953)
  blocking collectives: 72.4 us -> 41.5 us
    psum x1 -> x0, blocking collectives: 72.4 us -> none  [on_device(): column = lax.psum(jnp.sum(scaled, 0), 'tup')]
    all_gather x0 -> x1, blocking collectives: none -> 41.5 us  [on_device(): parts = lax.all_gather(own, 'tup')]
where the time goes in v1:
time: 631 us; the launch traced here: 629 us
  waiting for transfers between devices  439 us (70%)
  matrix products  49.9 us (8%)
  local copies, waits for them, and re-layouts  47.8 us (8%)
  blocking collectives  41.5 us (7%)
  starting transfers between devices  21.8 us (3%)
  other arithmetic  15.1 us (2%)
  between operations  13.8 us (2%)
    reduce_scatter x1, waiting for transfers between devices, ratio_pass(): lax.psum_scatter(word_sum, 'tup', scatter_dimension=0, tiled=True)  249 us
    all_to_all x1, waiting for transfers between devices, on_device(): lax.all_to_all(live_counts[bucket_order].reshape(groups, per_owner, vocab...  131 us
    psum x1, waiting for transfers between devices, on_device(): totals = lax.psum(placed, 'lang')  57.4 us
    all_gather x1, blocking collectives, on_device(): parts = lax.all_gather(own, 'tup')  41.5 us
    dot_general x8, matrix products, word_term(): lax.dot_general(ratios, mix_rows.astype(jnp.float32), (((0,), (0,)), ((),...  18.6 us
    dot_general x8, matrix products, topic_term(): jnp.dot(ratios, word_block.astype(jnp.float32), precision=lax.Precision.H...  18 us
    dot_general x8, matrix products, ratio_block(): lax.dot_general(mix_block, word_block, (((1,), (1,)), ((), ())), preferre...  13.3 us
  transfers between devices with their start and end apart: 5, of which 3 were waited for; matrix products, arithmetic and copies ran while one was open for 6% of the time, Pallas kernels for 0%

profile of v1, /device:TPU:4, one launch (start us, length us, event | category | flops | bytes accessed | tf_op | source)
XLA Modules:
  0.0 629.1 jit_solution(13690653622821734836)
XLA Ops:
  7.2 0.7 all-gather.5.cloned.1.call-update
  7.9 0.7 and_select_fusion.1
  8.6 2.5 sort.17
  11.1 1.6 gather_fusion
  12.7 0.7 all_to_all.9
  13.4 11.5 %all-to-all-start = ((s32[32,1,4]{2,1,0:T(1,128)}), s32[32,1,4]{2,1,0:T(1,128)S(1)}, u32[]{:S(2)}, u32[]{:S(2)}) async-start(s32[32,1,4]{2,1,0:T(1,128)} %bitcast.1), calls=%async_computation | async-start | bytes 32768 | tf_op jit(solution)/shard_map/all_to_all | solution.py:77
  24.9 5.4 compare_select_fusion
  30.3 11.5 %gather_fusion.1 = bf16[128,16384]{1,0:T(8,128)(2,1)} fusion(bf16[128,16384]{1,0:T(8,128)(2,1)} %compare_select_fusion, s32[1024]{0:T(1024)S(1)} %pad_clamp_fusion.1), kind=kCustom, calls=%fused_computation.1 | custom fusion | bytes 8389120 | tf_op jit(solution)/shard_map/gather | solution.py:71
  41.8 7.2 %reshape.96 = bf16[32,4,16384]{2,1,0:T(4,128)(2,1)} reshape(bf16[128,16384]{1,0:T(8,128)(2,1)} %gather_fusion.1) | data formatting | bytes 8388608 | tf_op jit(solution)/shard_map/reshape | solution.py:71
  49.1 10.0 %all-to-all-start.1 = ((bf16[32,4,16384]{2,1,0:T(4,128)(2,1)}), bf16[32,4,16384]{2,1,0:T(4,128)(2,1)}, u32[]{:S(2)}, u32[]{:S(2)}) async-start(bf16[32,4,16384]{2,1,0:T(4,128)(2,1)} %reshape.96), calls=%async_computation.1 | async-start | bytes 8388608 | tf_op jit(solution)/shard_map/all_to_all | solution.py:70
  59.4 0.5 broadcast.129
  59.9 0.7 reduce.4
  60.7 0.8 gather_fusion.2
  61.6 130.7 %all-to-all-done.1 = bf16[32,4,16384]{2,1,0:T(4,128)(2,1)} async-done(((bf16[32,4,16384]{2,1,0:T(4,128)(2,1)}), bf16[32,4,16384]{2,1,0:T(4,128)(2,1)}, u32[]{:S(2)}, u32[]{:S(2)}) %all-to-all-start.1) | async-done | bytes 4194336 | tf_op jit(solution)/shard_map/all_to_all | solution.py:70
  192.2 6.9 %reshape.97 = bf16[128,16384]{1,0:T(8,128)(2,1)} reshape(bf16[32,4,16384]{2,1,0:T(4,128)(2,1)} %all-to-all-done.1) | data formatting | bytes 8388608 | tf_op jit(solution)/shard_map/reshape | solution.py:76
  199.2 6.0 broadcast_in_dim.7
  205.2 60.9 %while.16 = (s32[]{:T(128)}, f32[128,256]{1,0:T(8,128)S(1)}, f32[16384,256]{1,0:T(8,128)}, bf16[128,16384]{1,0:T(8,128)(2,1)}, bf16[16384,256]{1,0:T(8,128)(2,1)...) while((s32[]{:T(128)}, f32[128,256]{1,0:T(8,128)S(1)}, ...), condition=%wide.region_2.3_spmd.clone, body=%wide.region_1.2_spmd.clone.sunk | while | flops 1745420288 | bytes 10354869 | solution.py:49
  205.2 1.1 constant_dynamic-slice_fusion.2
  206.2 0.3 copy.13
  206.5 1.7 fusion.31
  208.2 2.3 convolution_add_fusion.2
  210.4 2.3 convolution_dynamic-update-slice_fusion.2
  212.8 1.1 constant_dynamic-slice_fusion.2
  213.9 0.3 copy.13
  214.1 1.7 fusion.31
  215.8 2.3 convolution_add_fusion.2
  218.1 2.3 convolution_dynamic-update-slice_fusion.2
  220.3 1.1 constant_dynamic-slice_fusion.2
  221.4 0.3 copy.13
  221.7 1.7 fusion.31
  223.4 2.3 convolution_add_fusion.2
  225.6 2.3 convolution_dynamic-update-slice_fusion.2
  227.9 1.1 constant_dynamic-slice_fusion.2
  229.0 0.3 copy.13
  229.3 1.7 fusion.31
  231.0 2.3 convolution_add_fusion.2
  233.2 2.3 convolution_dynamic-update-slice_fusion.2
  235.6 1.1 constant_dynamic-slice_fusion.2
  236.6 0.3 copy.13
  236.9 1.7 fusion.31
  238.6 2.3 convolution_add_fusion.2
  240.9 2.4 convolution_dynamic-update-slice_fusion.2
  243.2 1.1 constant_dynamic-slice_fusion.2
  244.3 0.3 copy.13
  244.6 1.7 fusion.31
  246.3 2.3 convolution_add_fusion.2
  248.5 2.3 convolution_dynamic-update-slice_fusion.2
  250.8 1.1 constant_dynamic-slice_fusion.2
  252.2 1.7 fusion.31
  253.8 2.3 convolution_add_fusion.2
  256.1 2.3 convolution_dynamic-update-slice_fusion.2
  258.4 1.1 constant_dynamic-slice_fusion.2
  259.8 1.7 fusion.31
  261.5 2.3 convolution_add_fusion.2
  263.7 2.3 convolution_dynamic-update-slice_fusion.2
  266.0 1.6 scatter_custom_fusion
  267.7 0.7 reduce-scatter.2.cloned.1.call-update
  268.4 57.4 %all-reduce.2.cloned.1.call-done = f32[128,256]{1,0:T(8,128)} async-done(((f32[128,256]{1,0:T(8,128)}), f32[128,256]{1,0:T(8,128)}) %all-reduce.2.cloned.1.call-update) | async-done | bytes 131088 | tf_op jit(solution)/shard_map/psum | solution.py:84
  325.8 1.0 fusion.6
  326.8 1.7 multiply_divide_fusion
  328.5 249.4 %reduce-scatter.2.cloned.1.call-done = f32[512,256]{1,0:T(8,128)} async-done(((f32[16384,256]{1,0:T(8,128)}), f32[512,256]{1,0:T(8,128)}) %reduce-scatter.2.cloned.1.call-update) | async-done | bytes 524304 | tf_op jit(solution)/shard_map/reduce_scatter | solution.py:55
  577.9 1.1 fusion.5
  579.1 41.5 %all-gather.2 = f32[32,1,256]{2,1,0:T(1,128)S(1)} all-gather(f32[1,1,256]{2,1,0:T(1,128)S(1)} %bitcast.37), channel_id=3, replica_groups=mesh['tup'=32,'lang'=8] {'tup'}, dimensions={0}, use_global_device_ids=true | all-gather | bytes 33792 | tf_op jit(solution)/shard_map/all_gather | solution.py:89
  620.6 1.9 divide_bitcast_fusion
  (21 shorter events, 1.1 us)
Async XLA Ops:
  7.2 192.0 %all-gather.5.cloned.1.call-start = ((), (), s32[]{:S(2)}) async-start(), calls=%async_computation.5 | async-start | bytes 8650752 | tf_op jit(solution)/shard_map/all_gather | solution.py:33
  13.4 35.6 %all-to-all-start = ((s32[32,1,4]{2,1,0:T(1,128)}), s32[32,1,4]{2,1,0:T(1,128)S(1)}, u32[]{:S(2)}, u32[]{:S(2)}) async-start(s32[32,1,4]{2,1,0:T(1,128)} %bitcast.1), calls=%async_computation | async-start | bytes 32768 | tf_op jit(solution)/shard_map/all_to_all | solution.py:77
  49.1 11.6 %copy-start = (bf16[128,256]{1,0:T(8,128)(2,1)S(1)}, bf16[128,256]{1,0:T(8,128)(2,1)}, u32[]{:S(2)}) copy-start(bf16[128,256]{1,0:T(8,128)(2,1)} %param.10) | copy-start | bytes 196612
  49.1 143.2 %all-to-all-start.1 = ((bf16[32,4,16384]{2,1,0:T(4,128)(2,1)}), bf16[32,4,16384]{2,1,0:T(4,128)(2,1)}, u32[]{:S(2)}, u32[]{:S(2)}) async-start(bf16[32,4,16384]{2,1,0:T(4,128)(2,1)} %reshape.96), calls=%async_computation.1 | async-start | bytes 8388608 | tf_op jit(solution)/shard_map/all_to_all | solution.py:70
  59.1 266.7 %all-reduce.2.cloned.1.call-start = ((), (), s32[]{:S(2)}) async-start(), calls=%async_computation.3 | async-start | bytes 262144 | tf_op jit(solution)/shard_map/psum | solution.py:84
  267.7 310.2 %reduce-scatter.2.cloned.1.call-start = ((), (), s32[]{:S(2)}) async-start(), calls=%async_computation.4 | async-start | bytes 17301504 | tf_op jit(solution)/shard_map/reduce_scatter | solution.py:55
  267.7 310.2 %copy-start.1 = (bf16[1,512,256]{2,1,0:T(8,128)(2,1)S(1)}, bf16[1,512,256]{2,1,0:T(8,128)(2,1)}, u32[]{:S(2)}) copy-start(bf16[1,512,256]{2,1,0:T(8,128)(2,1)} %param.11) | copy-start | bytes 786436
Sparse Core Ops, SparseCore 0:
  10.6 176.9 all-gather.4
  267.8 57.9 all-reduce.1
  330.5 247.3 reduce-scatter.1
